TPU v7x, 256 devices: a whole 4x4x8 slice. The times are simulated.
256 devices in a mesh: dom: 128 (over x, y, z), rep: 2 (over core).
Axes of the slice: x: 4, y: 4, z: 8, core: 2. Of those that a mesh axis runs over, the one named last changes fastest.
Arguments:
- features: bfloat16 [131072, 256], P(('dom', 'rep')), may hold values from -6 to 6
- w_self: bfloat16 [256, 256], replicated, may hold values from -0.375 to 0.375
- w_neigh: bfloat16 [256, 256], replicated, may hold values from -0.375 to 0.375
- bias_vector: float32 [256], replicated, may hold values from -3 to 3
- upstream: bfloat16 [131072, 256], P(('dom', 'rep')), may hold values from -6 to 6
- sources: int32 [1048576], P(('dom', 'rep')), may hold values from 0 to 1023
- edge_slots: int32 [1048576], P(('dom', 'rep')), may hold values from 0 to 2047, as said below
- mirror_rows: int32 [128, 128, 16], P('dom'), may hold values from 0 to 1023, as said below
Outputs:
- hidden: bfloat16 [131072, 256], P(('dom', 'rep'))
- input_grad: bfloat16 [131072, 256], P(('dom', 'rep'))
- grad_self: float32 [256, 256], replicated
- grad_neigh: float32 [256, 256], replicated
- grad_bias: float32 [256], replicated
Inputs may be any that keep to these rules, and one draw needn't show every extreme that they name: `edge_slots`: slot s stands for column s % 16 of partition s // 16. mirror_rows[q, p, c] is a master row of partition q; the 16 rows of one [q, p] are different.
All inputs are finite; a program needn't handle non-finite values.
Results may differ from a plain program's by a relative error of at most 0.007.
Values may be sent and summed in bfloat16 or wider, within the bound.
A program may use at most 64 MiB of HBM per device.

v0:
```python
import math

import jax
import jax.numpy as jnp
from jax import lax
from jax.sharding import PartitionSpec as P


def one_hot_rows(indices, count, dtype):
    return (indices[:, None] == jnp.arange(count, dtype=jnp.int32)[None, :]).astype(dtype)


def edge_partials(part_rows, sources, edge_slots, slot_count):
    feat_width = part_rows.shape[1]
    block_size = min(2048, sources.shape[0])
    source_blocks = sources.reshape(-1, block_size)
    slot_blocks = edge_slots.reshape(-1, block_size)
    dims = (((0,), (0,)), ((), ()))

    def block_step(running, inputs):
        summed, counted = running
        source_block, slot_block = inputs
        picked = part_rows[source_block]
        selector = one_hot_rows(slot_block, slot_count, jnp.bfloat16)
        summed = summed + lax.dot_general(
            selector, picked, dims, preferred_element_type=jnp.float32
        )
        counted = counted + jnp.sum(selector, axis=0, dtype=jnp.float32)
        return ((summed, counted), None)

    start = (
        jnp.zeros((slot_count, feat_width), jnp.float32),
        jnp.zeros((slot_count,), jnp.float32),
    )
    result, _ = lax.scan(block_step, start, (source_blocks, slot_blocks))
    return result


def edge_returns(slot_grads, sources, edge_slots, row_count):
    feat_width = slot_grads.shape[1]
    block_size = min(2048, sources.shape[0])
    source_blocks = sources.reshape(-1, block_size)
    slot_blocks = edge_slots.reshape(-1, block_size)
    dims = (((0,), (0,)), ((), ()))

    def block_step(running, inputs):
        source_block, slot_block = inputs
        picked = slot_grads[slot_block]
        selector = one_hot_rows(source_block, row_count, jnp.bfloat16)
        return (
            running + lax.dot_general(selector, picked, dims, preferred_element_type=jnp.float32),
            None,
        )

    result, _ = lax.scan(
        block_step, jnp.zeros((row_count, feat_width), jnp.float32), (source_blocks, slot_blocks)
    )
    return result


def place_rows(values, counts, targets, row_count):
    selector = one_hot_rows(targets, row_count, jnp.float32)
    dims = (((0,), (0,)), ((), ()))
    placed = lax.dot_general(
        selector, values, dims, preferred_element_type=jnp.float32, precision=lax.Precision.HIGHEST
    )
    placed_counts = jnp.dot(
        counts, selector, preferred_element_type=jnp.float32, precision=lax.Precision.HIGHEST
    )
    return (placed, placed_counts)


def shards(features, w_self, w_neigh, bias_vector, upstream, sources, edge_slots, mirror_rows):
    dom_count = lax.axis_size("dom")
    rep_count = lax.axis_size("rep")
    feat_width = features.shape[1]
    own_count = features.shape[0]
    part_rows = lax.all_gather(features, "rep", axis=0, tiled=True)
    row_count = part_rows.shape[0]
    mirror_map = mirror_rows[0]
    slot_width = mirror_map.shape[1]
    slot_count = dom_count * slot_width
    partial_sums, partial_counts = edge_partials(part_rows, sources, edge_slots, slot_count)
    slot_sums = partial_sums.reshape(dom_count, slot_width, feat_width)
    slot_counts = partial_counts.reshape(dom_count, slot_width)
    arrived, arrived_counts = (
        lax.all_to_all(slot_sums, "dom", split_axis=0, concat_axis=0, tiled=True),
        lax.all_to_all(slot_counts, "dom", split_axis=0, concat_axis=0, tiled=True),
    )
    flat_targets = mirror_map.reshape(-1)
    part_sums, part_degree = place_rows(
        arrived.reshape(-1, feat_width), arrived_counts.reshape(-1), flat_targets, row_count
    )
    neigh_sum, degree = (
        lax.psum_scatter(part_sums, "rep", scatter_dimension=0, tiled=True),
        lax.psum_scatter(part_degree, "rep", scatter_dimension=0, tiled=True),
    )
    divisor = jnp.maximum(degree, 1.0)[:, None]
    neigh_mean = (neigh_sum / divisor).astype(jnp.bfloat16)
    pre = (
        jnp.dot(features, w_self, preferred_element_type=jnp.float32)
        + jnp.dot(neigh_mean, w_neigh, preferred_element_type=jnp.float32)
        + bias_vector
    )
    sigma = jax.nn.sigmoid(pre)
    hidden = (pre * sigma).astype(jnp.bfloat16)
    pre_grad = (upstream.astype(jnp.float32) * (sigma + pre * sigma * (1.0 - sigma))).astype(
        jnp.bfloat16
    )
    dims = (((0,), (0,)), ((), ()))
    self_term = lax.dot_general(features, pre_grad, dims, preferred_element_type=jnp.float32)
    neigh_term = lax.dot_general(neigh_mean, pre_grad, dims, preferred_element_type=jnp.float32)
    bias_term = jnp.sum(pre_grad.astype(jnp.float32), axis=0)
    self_total, neigh_total, bias_total = lax.psum(
        (self_term, neigh_term, bias_term), ("dom", "rep")
    )
    grad_scale = 1.0 / math.sqrt(dom_count * rep_count * own_count)
    mean_grad = (jnp.dot(pre_grad, w_neigh.T, preferred_element_type=jnp.float32) / divisor).astype(
        jnp.bfloat16
    )
    self_grad = jnp.dot(pre_grad, w_self.T, preferred_element_type=jnp.float32)
    part_grads = lax.all_gather(mean_grad, "rep", axis=0, tiled=True)
    slot_grads = lax.all_to_all(
        part_grads[mirror_map], "dom", split_axis=0, concat_axis=0, tiled=True
    )
    flat_grads = slot_grads.reshape(slot_count, feat_width)
    edge_grads = edge_returns(flat_grads, sources, edge_slots, row_count)
    owned_grads = lax.psum_scatter(edge_grads, "rep", scatter_dimension=0, tiled=True)
    input_grad = (self_grad + owned_grads).astype(jnp.bfloat16)
    return (
        hidden,
        input_grad,
        self_total * grad_scale,
        neigh_total * grad_scale,
        bias_total * grad_scale,
    )


def solution(mesh):
    in_specs = (
        P(("dom", "rep"), None),
        P(),
        P(),
        P(),
        P(("dom", "rep"), None),
        P(("dom", "rep")),
        P(("dom", "rep")),
        P("dom", None, None),
    )
    out_specs = (P(("dom", "rep"), None), P(("dom", "rep"), None), P(), P(), P())
    return jax.shard_map(shards, mesh=mesh, in_specs=in_specs, out_specs=out_specs, check_vma=False)
```

profile of v0, /device:TPU:1, one launch (start us, length us, event | category | flops | bytes accessed | tf_op | source)
XLA Modules:
  0.0 455.7 jit_solution(8431748517340846413)
XLA Ops:
  7.2 0.8 reshape.126
  8.0 0.7 reshape.127
  8.7 5.3 %all_gather.6 = bf16[1024,256]{1,0:T(8,128)(2,1)S(1)} all-gather(bf16[512,256]{1,0:T(8,128)(2,1)} %param.12), channel_id=1, replica_groups=mesh['dom'=128,'rep'=2] {'rep'}, dimensions={0}, use_global_device_ids=true | all-gather | bytes 786432 | tf_op jit(solution)/shard_map/all_gather | solution.py:78
  14.0 33.3 %while.24 = (s32[]{:T(128)}, f32[2048,256]{1,0:T(8,128)}, f32[2048]{0:T(1024)S(1)}, s32[2,2048]{1,0:T(2,128)S(1)}, s32[2,2048]{1,0:T(2,128)S(1)}, /*index=5*/bf16[1024,256]{1,0:T(8,128)(2,1)S(1)}, s32[]{:T(128)}, s32[]{:T(128)}) while((s32[]{:T(128)}, f32[2048,256]{1,0:T(8,128)}, f32[2048]{0:T(1024)S(1)}, s32[2,2048]{1,0:T(2,128)S(1)}, ...), condition=%wide.region_2.3_spmd.clone, body=%wide.region_0.2_spmd.clone.sunk | while | flops 2169513984 | bytes 7446632 | solution.py:35
  14.0 7.5 %gather_fusion = bf16[2048,256]{1,0:T(8,128)(2,1)S(1)} fusion(bf16[1024,256]{1,0:T(8,128)(2,1)S(1)} %get-tuple-element.245, s32[2048]{0:T(1024)S(1)} %broadcast_clamp_fusion.5), kind=kCustom, calls=%fused_computation.clone.clone.1 | custom fusion | bytes 2105344 | tf_op jit(solution)/shard_map/while/body/eval_jaxpr/gather | solution.py:23
  21.5 6.2 %fusion.39 = f32[2048,256]{1,0:T(8,128)} fusion(bf16[2048,256]{1,0:T(8,128)(2,1)S(1)} %gather_fusion, s32[2048]{0:T(1024)S(1)} %bitcast.58, f32[2048,256]{1,0:T(8,128)} %get-tuple-element.233, pred[]{:T(512)S(6)} %compare.6), kind=kOutput, calls=%fused_computation.8.clone.1 | convolution fusion | flops 2152726528 | bytes 5251073 | tf_op jit(solution)/shard_map/while/body/eval_jaxpr/dot_general | solution.py:25
  27.7 2.1 convert_reduce_fusion.3
  29.9 7.5 %gather_fusion = bf16[2048,256]{1,0:T(8,128)(2,1)S(1)} fusion(bf16[1024,256]{1,0:T(8,128)(2,1)S(1)} %get-tuple-element.245, s32[2048]{0:T(1024)S(1)} %broadcast_clamp_fusion.5), kind=kCustom, calls=%fused_computation.clone.clone.1 | custom fusion | bytes 2105344 | tf_op jit(solution)/shard_map/while/body/eval_jaxpr/gather | solution.py:23
  37.4 7.8 %fusion.39 = f32[2048,256]{1,0:T(8,128)} fusion(bf16[2048,256]{1,0:T(8,128)(2,1)S(1)} %gather_fusion, s32[2048]{0:T(1024)S(1)} %bitcast.58, f32[2048,256]{1,0:T(8,128)} %get-tuple-element.233, pred[]{:T(512)S(6)} %compare.6), kind=kOutput, calls=%fused_computation.8.clone.1 | convolution fusion | flops 2152726528 | bytes 5251073 | tf_op jit(solution)/shard_map/while/body/eval_jaxpr/dot_general | solution.py:25
  45.2 2.1 convert_reduce_fusion.3
  47.3 13.8 %all-to-all-start = ((f32[128,16,256]{2,1,0:T(8,128)}), f32[128,16,256]{2,1,0:T(8,128)S(1)}, u32[]{:S(2)}, u32[]{:S(2)}) async-start(f32[128,16,256]{2,1,0:T(8,128)} %bitcast.55), calls=%async_computation | async-start | bytes 4194304 | tf_op jit(solution)/shard_map/all_to_all | solution.py:87
  61.1 0.2 reduce-scatter.3.cloned.1.call-start
  61.3 0.1 copy.27
  61.5 52.5 %all-to-all-done = f32[128,16,256]{2,1,0:T(8,128)S(1)} async-done(((f32[128,16,256]{2,1,0:T(8,128)}), f32[128,16,256]{2,1,0:T(8,128)S(1)}, u32[]{:S(2)}, u32[]{:S(2)}) %all-to-all-start) | async-done | bytes 2097184 | tf_op jit(solution)/shard_map/all_to_all | solution.py:87
  114.0 8.0 %fusion.8 = f32[1024,256]{1,0:T(8,128)} fusion(f32[2048,256]{1,0:T(8,128)S(1)} %bitcast.54, s32[2048]{0:T(1024)S(1)} %eq.45), kind=kOutput, calls=%fused_computation.22 | convolution fusion | flops 6444548096 | bytes 3153920 | tf_op jit(solution)/shard_map/dot_general | solution.py:64
  122.0 0.7 all_to_all.13
  122.7 6.1 %all-to-all-start.1 = ((f32[128,1,16]{2,1,0:T(1,128)}), f32[128,1,16]{2,1,0:T(1,128)S(1)}, u32[]{:S(2)}, u32[]{:S(2)}) async-start(f32[128,1,16]{2,1,0:T(1,128)} %bitcast.2), calls=%async_computation.2 | async-start | bytes 131072 | tf_op jit(solution)/shard_map/all_to_all | solution.py:88
  128.9 0.1 copy.29
  129.1 0.2 fusion.16
  129.4 0.6 dynamic-slice
  130.6 8.8 %all-to-all-done.1 = f32[128,1,16]{2,1,0:T(1,128)S(1)} async-done(((f32[128,1,16]{2,1,0:T(1,128)}), f32[128,1,16]{2,1,0:T(1,128)S(1)}, u32[]{:S(2)}, u32[]{:S(2)}) %all-to-all-start.1) | async-done | bytes 8224 | tf_op jit(solution)/shard_map/all_to_all | solution.py:88
  139.4 0.5 broadcast.109
  139.9 0.8 reduce.3
  140.7 0.1 reshape.163
  140.8 2.7 fusion.7
  143.5 5.7 %all-reduce = f32[1024]{0:T(1024)S(1)} all-reduce(f32[1024]{0:T(1024)S(1)} %bitcast.61), channel_id=3, replica_groups=mesh['dom'=128,'rep'=2] {'rep'}, use_global_device_ids=true, to_apply=%region_4.5.clone | all-reduce | flops 1024 | bytes 8192
  149.3 1.2 divide_convert_fusion
  150.5 1.1 convert_reduce_fusion.1
  151.7 0.3 fusion.13
  151.9 2.2 all_gather.7
  154.1 9.0 %gather_fusion.2 = bf16[2048,256]{1,0:T(8,128)(2,1)} fusion(bf16[1024,256]{1,0:T(8,128)(2,1)S(1)} %all_gather.7, s32[2048]{0:T(1024)S(1)} %broadcast_clamp_fusion.2), kind=kCustom, calls=%fused_computation.2 | custom fusion | bytes 2105344 | tf_op jit(solution)/shard_map/gather | solution.py:124
  163.1 6.2 %all-to-all-start.2 = ((bf16[128,16,256]{2,1,0:T(8,128)(2,1)}), bf16[128,16,256]{2,1,0:T(8,128)(2,1)S(1)}, u32[]{:S(2)}, u32[]{:S(2)}) async-start(bf16[128,16,256]{2,1,0:T(8,128)(2,1)} %bitcast.5), calls=%async_computation.3 | async-start | bytes 2097152 | tf_op jit(solution)/shard_map/all_to_all | solution.py:123
  169.4 1.0 fusion.17
  170.4 1.0 convolution_bitcast_fusion
  171.4 29.0 %all-to-all-done.2 = bf16[128,16,256]{2,1,0:T(8,128)(2,1)S(1)} async-done(((bf16[128,16,256]{2,1,0:T(8,128)(2,1)}), bf16[128,16,256]{2,1,0:T(8,128)(2,1)S(1)}, u32[]{:S(2)}, u32[]{:S(2)}) %all-to-all-start.2) | async-done | bytes 1048608 | tf_op jit(solution)/shard_map/all_to_all | solution.py:123
  200.4 23.7 %while.25 = (s32[]{:T(128)}, f32[1024,256]{1,0:T(8,128)}, s32[2,2048]{1,0:T(2,128)S(1)}, s32[2,2048]{1,0:T(2,128)S(1)}, bf16[2048,256]{1,0:T(8,128)(2,1)S(1)}, /*index=5*/s32[]{:T(128)}, s32[]{:T(128)}) while((s32[]{:T(128)}, f32[1024,256]{1,0:T(8,128)}, s32[2,2048]{1,0:T(2,128)S(1)}, s32[2,2048]{1,0:T(2,128)S(1)}, ...), condition=%wide.region_6.7_spmd.clone, body=%wide.region_5.6_spmd.clone.sunk | while | flops 1076371456 | bytes 5308511 | solution.py:55
  200.5 7.5 %gather_fusion.1 = bf16[2048,256]{1,0:T(8,128)(2,1)S(1)} fusion(bf16[2048,256]{1,0:T(8,128)(2,1)S(1)} %get-tuple-element.266, s32[2048]{0:T(1024)S(1)} %broadcast_clamp_fusion.6), kind=kCustom, calls=%fused_computation.1.clone.clone.1 | custom fusion | bytes 2105344 | tf_op jit(solution)/shard_map/while/body/eval_jaxpr/gather | solution.py:48
  208.0 3.7 fusion.41
  211.7 7.5 %gather_fusion.1 = bf16[2048,256]{1,0:T(8,128)(2,1)S(1)} fusion(bf16[2048,256]{1,0:T(8,128)(2,1)S(1)} %get-tuple-element.266, s32[2048]{0:T(1024)S(1)} %broadcast_clamp_fusion.6), kind=kCustom, calls=%fused_computation.1.clone.clone.1 | custom fusion | bytes 2105344 | tf_op jit(solution)/shard_map/while/body/eval_jaxpr/gather | solution.py:48
  219.3 4.9 %fusion.41 = f32[1024,256]{1,0:T(8,128)} fusion(bf16[2048,256]{1,0:T(8,128)(2,1)S(1)} %gather_fusion.1, s32[2048]{0:T(1024)S(1)} %bitcast.60, f32[1024,256]{1,0:T(8,128)} %get-tuple-element.256, pred[]{:T(512)S(6)} %compare.7), kind=kOutput, calls=%fused_computation.16.clone.1 | convolution fusion | flops 1076363264 | bytes 3153921 | tf_op jit(solution)/shard_map/while/body/eval_jaxpr/dot_general | solution.py:51
  224.2 72.9 %psum.23 = f32[256]{0:T(256)S(1)} all-reduce(f32[256]{0:T(256)S(1)} %get-tuple-element.151), channel_id=1, replica_groups=mesh['dom'=128,'rep'=2] {'dom','rep'}, use_global_device_ids=true, to_apply=%region_11.12 | all-reduce | flops 256 | bytes 2048 | tf_op jit(solution)/shard_map/psum | solution.py:114
  297.1 0.6 broadcast_multiply_fusion.2
  297.7 132.0 %all-reduce.4.cloned.1.call-done = (f32[256,256]{0,1:T(8,128)}, f32[256,256]{0,1:T(8,128)}) async-done(((f32[256,256]{0,1:T(8,128)}, f32[256,256]{0,1:T(8,128)}), (f32[256,256]{0,1:T(8,128)}, f32[256,256]{0,1:T(8,128)})) %all-reduce.4.cloned.1.call-update) | async-done | bytes 524304 | tf_op jit(solution)/shard_map/psum | solution.py:114
  429.7 1.1 broadcast_multiply_fusion
  430.8 0.8 copy.31
  431.6 0.8 copy.32
  432.4 14.7 %reduce-scatter.5.cloned.1.call-done = f32[512,256]{1,0:T(8,128)} async-done(((f32[1024,256]{1,0:T(8,128)}), f32[512,256]{1,0:T(8,128)}) %reduce-scatter.5.cloned.1.call-update) | async-done | bytes 524304 | tf_op jit(solution)/shard_map/reduce_scatter | solution.py:128
  447.1 2.0 fusion.12
  (42 shorter events, 0.6 us)
Async XLA Ops:
  7.2 143.4 %copy-start = (bf16[256,256]{1,0:T(8,128)(2,1)S(1)}, bf16[256,256]{1,0:T(8,128)(2,1)}, u32[]{:S(2)}) copy-start(bf16[256,256]{1,0:T(8,128)(2,1)} %param.14) | copy-start | bytes 393220
  47.3 14.0 %copy-start.3 = (s32[1,128,16]{1,2,0:T(8,128)S(1)}, s32[1,128,16]{1,2,0:T(8,128)}, u32[]{:S(2)}) copy-start(s32[1,128,16]{1,2,0:T(8,128)} %param.19) | copy-start | bytes 24580
  47.3 66.7 %all-to-all-start = ((f32[128,16,256]{2,1,0:T(8,128)}), f32[128,16,256]{2,1,0:T(8,128)S(1)}, u32[]{:S(2)}, u32[]{:S(2)}) async-start(f32[128,16,256]{2,1,0:T(8,128)} %bitcast.55), calls=%async_computation | async-start | bytes 4194304 | tf_op jit(solution)/shard_map/all_to_all | solution.py:87
  61.1 88.2 %reduce-scatter.3.cloned.1.call-start = ((), (), s32[]{:S(2)}) async-start(), calls=%async_computation.5 | async-start | bytes 1572864 | tf_op jit(solution)/shard_map/reduce_scatter | solution.py:95
  114.0 15.1 %copy-start.1 = (bf16[512,256]{1,0:T(8,128)(2,1)S(1)}, bf16[512,256]{1,0:T(8,128)(2,1)}, u32[]{:S(2)}) copy-start(bf16[512,256]{1,0:T(8,128)(2,1)} %param.12) | copy-start | bytes 786436
  114.0 15.1 %copy-start.2 = (bf16[256,256]{1,0:T(8,128)(2,1)S(1)}, bf16[256,256]{1,0:T(8,128)(2,1)}, u32[]{:S(2)}) copy-start(bf16[256,256]{1,0:T(8,128)(2,1)} %param.13) | copy-start | bytes 393220
  122.0 7.4 %copy-start.6 = (u32[256]{0:T(256)S(1)}, u32[256]{0:T(256)}, u32[]{:S(2)}) copy-start(u32[256]{0:T(256)} %constant.42) | copy-start | bytes 3076
  122.7 16.6 %all-to-all-start.1 = ((f32[128,1,16]{2,1,0:T(1,128)}), f32[128,1,16]{2,1,0:T(1,128)S(1)}, u32[]{:S(2)}, u32[]{:S(2)}) async-start(f32[128,1,16]{2,1,0:T(1,128)} %bitcast.2), calls=%async_computation.2 | async-start | bytes 131072 | tf_op jit(solution)/shard_map/all_to_all | solution.py:88
  129.0 21.5 %copy-start.4 = (bf16[512,256]{1,0:T(8,128)(2,1)S(1)}, bf16[512,256]{1,0:T(8,128)(2,1)}, u32[]{:S(2)}) copy-start(bf16[512,256]{1,0:T(8,128)(2,1)} %param.16) | copy-start | bytes 786436
  129.0 21.5 %copy-start.5 = (f32[256]{0:T(256)S(1)}, f32[256]{0:T(256)}, u32[]{:S(2)}) copy-start(f32[256]{0:T(256)} %param.15) | copy-start | bytes 3076
  163.1 37.3 %all-to-all-start.2 = ((bf16[128,16,256]{2,1,0:T(8,128)(2,1)}), bf16[128,16,256]{2,1,0:T(8,128)(2,1)S(1)}, u32[]{:S(2)}, u32[]{:S(2)}) async-start(bf16[128,16,256]{2,1,0:T(8,128)(2,1)} %bitcast.5), calls=%async_computation.3 | async-start | bytes 2097152 | tf_op jit(solution)/shard_map/all_to_all | solution.py:123
  169.3 260.3 %all-reduce.4.cloned.1.call-start = ((), (), s32[]{:S(2)}) async-start(), calls=%async_computation.7 | async-start | bytes 1048576 | tf_op jit(solution)/shard_map/psum | solution.py:114
  171.4 275.8 %reduce-scatter.5.cloned.1.call-start = ((), (), s32[]{:S(2)}) async-start(), calls=%async_computation.6 | async-start | bytes 1572864 | tf_op jit(solution)/shard_map/reduce_scatter | solution.py:128
Sparse Core Ops, SparseCore 0:
  122.1 8.5 reduce-scatter.2
  177.3 252.3 all-reduce.3
  432.3 14.7 reduce-scatter.4
where the time goes:
time: 456 us
  waiting for transfers between devices  237 us (52%)
  blocking collectives  86.1 us (19%)
  local copies, waits for them, and re-layouts  44.5 us (10%)
  matrix products  38.9 us (9%)
  starting transfers between devices  26.4 us (6%)
  between operations  14.6 us (3%)
  other arithmetic  7.94 us (2%)
    psum x1, waiting for transfers between devices, shards(): lax.psum((self_term, neigh_term, bias_term), ('dom', 'rep'))  132 us
    psum x1, blocking collectives, shards(): lax.psum((self_term, neigh_term, bias_term), ('dom', 'rep'))  72.9 us
    all_to_all x1, waiting for transfers between devices, shards(): lax.all_to_all(slot_sums, 'dom', split_axis=0, concat_axis=0, tiled=True)  52.5 us
    all_to_all x1, waiting for transfers between devices, shards(): lax.all_to_all(part_grads[mirror_map], 'dom', split_axis=0, concat_axis=0...  29 us
    dot_general x4, matrix products, block_step(): lax.dot_general(selector, picked, dims, preferred_element_type=jnp.float32)  22.6 us
    gather x2, local copies, waits for them, and re-layouts, block_step(): picked = part_rows[source_block]  15 us
    gather x2, local copies, waits for them, and re-layouts, block_step(): picked = slot_grads[slot_block]  15 us
    reduce_scatter x1, waiting for transfers between devices, shards(): lax.psum_scatter(edge_grads, 'rep', scatter_dimension=0, tiled=True)  14.7 us
  transfers between devices with their start and end apart: 6, of which 5 were waited for; matrix products, arithmetic and copies ran while one was open for 8% of the time, Pallas kernels for 0%

commit v1 on v0

v1 whole, which is shorter than its diff:
```python
import functools
import math

import jax
import jax.numpy as jnp
from jax import lax
from jax.experimental import pallas as pl
from jax.experimental.pallas import tpu as pltpu
from jax.sharding import PartitionSpec as P

MESH = pl.DeviceIdType.MESH
BF = jnp.bfloat16
F32 = jnp.float32
F8 = jnp.float8_e4m3fn

NN = (((1,), (0,)), ((), ()))
NT = (((1,), (1,)), ((), ()))
TN = (((0,), (0,)), ((), ()))

CHUNK = 2048
BLOCK = 256
MSG = 16


def dot(a, b, dims=NN):
    return lax.dot_general(a, b, dims, preferred_element_type=F32)


def one_hot_cols(index_row, count, dtype):
    n = index_row.shape[1]
    rows = lax.broadcasted_iota(jnp.int32, (count, n), 0).astype(jnp.int16)
    wanted = jnp.broadcast_to(index_row, (count, n)).astype(jnp.int16)
    return jnp.where(rows == wanted, jnp.ones((), BF), jnp.zeros((), BF)).astype(dtype)


def rows_at(start, count, unit):
    return pl.ds(pl.multiple_of(start, unit), count)


def kernel(
    feat, w_self, w_neigh, bias, up, src, slot, mir,
    hidden, igrad, gself, gneigh, gbias,
    psrc, pslot, fall, ssrc, at, sums, cnt, recv_f, crecv,
    pt, pm, nsum, nrecv, dpart, drecv, mg, gsend, recv_b, esum, erecv, selfg,
    term, trecv, rs, zr, ag, bb, bz, b2,
    rep_send, rep_recv, fs_sem, fr_sem, cs_sem, cr_sem, bs_sem, br_sem,
    ar_send, ar_recv,
):
    p = lax.axis_index("dom")
    r = lax.axis_index("rep")
    o = 1 - r
    x, y, z = p // 32, (p // 8) % 4, p % 8
    h, a, b = x // 2, x % 2, y // 2
    m = x * 4 + y
    my_idx = (a * 4 + y) * 8 + z
    is_home = h == r

    bar = pltpu.get_barrier_semaphore()

    def tell(dom, rep):
        pl.semaphore_signal(bar, inc=1, device_id=(dom, rep), device_id_type=MESH)

    tell(p, o)

    def tell_half(k, c):
        @pl.when(jnp.logical_not(jnp.logical_and(is_home, k == my_idx)))
        def _():
            tell(r * 64 + k, h)

        return c

    lax.fori_loop(0, 64, tell_half, 0)
    lax.fori_loop(1, 16, lambda k, c: (tell(((m + k) % 16) * 8 + z, r), c)[1], 0)
    lax.fori_loop(1, 8, lambda k, c: (tell(m * 8 + (z + k) % 8, r), c)[1], 0)

    own_rows = rows_at(r * 512, 512, 512)
    other_rows = rows_at(o * 512, 512, 512)

    for c in range(2):
        ssrc[c] = one_hot_cols(src[:, c * CHUNK:(c + 1) * CHUNK], 1024, F8)
    fall[own_rows, :] = feat[...]

    pl.semaphore_wait(bar, 87 - jnp.where(is_home, 1, 0))

    def to_other(source, target, n):
        return pltpu.make_async_remote_copy(
            source, target, rep_send.at[n], rep_recv.at[n],
            device_id=(p, o), device_id_type=MESH,
        )

    c_src = to_other(src, psrc, 0)
    c_slot = to_other(slot, pslot, 1)
    c_feat = to_other(feat, fall.at[own_rows, :], 2)
    c_src.start()
    c_slot.start()
    c_feat.start()
    c_src.wait_recv()
    for c in range(2):
        ssrc[2 + c] = one_hot_cols(psrc[:, c * CHUNK:(c + 1) * CHUNK], 1024, F8)
    c_slot.wait_recv()

    def send_block(t, source, target, send_sem, recv_sem, counts):
        i, j = (a + t // 2) % 2, (b + t % 2) % 2

        def step(k, c):
            line = i * 4 + 2 * j + k // 8
            idx = line * 8 + (z + k) % 8
            here = rows_at(idx * MSG, MSG, MSG)
            there = rows_at(my_idx * MSG, MSG, MSG)
            is_self = jnp.logical_and(is_home, idx == my_idx)

            @pl.when(jnp.logical_not(is_self))
            def _():
                dev = (r * 64 + idx, h)
                if counts:
                    pltpu.make_async_remote_copy(
                        cnt.at[line], crecv.at[my_idx], cs_sem, cr_sem,
                        device_id=dev, device_id_type=MESH,
                    ).start()
                pltpu.make_async_remote_copy(
                    source.at[here, :], target.at[there, :], send_sem, recv_sem.at[t],
                    device_id=dev, device_id_type=MESH,
                ).start()

            @pl.when(is_self)
            def _():
                if counts:
                    pltpu.make_async_copy(cnt.at[line], crecv.at[my_idx], cr_sem).start()
                pltpu.make_async_copy(source.at[here, :], target.at[there, :], recv_sem.at[t]).start()

            return c

        lax.fori_loop(0, 16, step, 0)

    def block_of(t):
        return (a + t // 2) % 2 * 2 + (b + t % 2) % 2

    def wait_block(t, target, recv_sem):
        part = target.at[rows_at(block_of(t) * BLOCK, BLOCK, BLOCK), :]
        pltpu.make_async_copy(part, part, recv_sem.at[t]).wait()

    for t in range(4):
        blk = block_of(t)
        base = r * 1024 + blk * BLOCK
        acc = None
        for c in range(4):
            row = slot if c < 2 else pslot
            lo = (c % 2) * CHUNK
            sel = one_hot_cols(row[:, lo:lo + CHUNK] - base, BLOCK, F8)
            d = dot(ssrc[c], sel, NT)
            acc = d if acc is None else acc + d
        counted = jnp.sum(acc, axis=0, keepdims=True)
        cnt[blk * 2] = counted[:, :128]
        cnt[blk * 2 + 1] = counted[:, 128:]
        table = acc.astype(BF)
        at[blk] = table
        if t == 0:
            c_feat.wait_recv()
        sums[rows_at(blk * BLOCK, BLOCK, BLOCK), :] = dot(table, fall[...], TN).astype(BF)
        send_block(t, sums, recv_f, fs_sem, fr_sem, True)

    mirror = mir[rows_at(r * 64, 64, 64), :]
    spread = jnp.broadcast_to(mirror[:, None, :], (64, 16, 16)).reshape(1024, 16)
    lane = lax.broadcasted_iota(jnp.int32, (1024, 16), 1)
    sub = lax.broadcasted_iota(jnp.int32, (1024, 16), 0)
    col = jnp.sum(jnp.where(lane == sub % 16, spread, 0), axis=1, keepdims=True)
    for q in range(4):
        part = col[q * BLOCK:(q + 1) * BLOCK]
        hit = lax.broadcasted_iota(jnp.int32, (BLOCK, 1024), 1) == part
        pt[q] = jnp.where(hit, 1.0, 0.0).astype(BF)
        row = jnp.broadcast_to(part.astype(F32), (BLOCK, 128)).T[0:1].astype(jnp.int32)
        pm[q] = one_hot_cols(row, 1024, BF)

    pre_self = dot(feat[...], w_self[...]) + bias[...]

    pltpu.make_async_copy(crecv, crecv, cr_sem).wait()
    got = crecv[...].reshape(64, 128)
    wide = jnp.broadcast_to(got[:, None, :], (64, 16, 128)).reshape(1024, 128)
    lane = lax.broadcasted_iota(jnp.int32, (1024, 128), 1)
    sub = lax.broadcasted_iota(jnp.int32, (1024, 128), 0)
    wide = jnp.where(lane == z * 16 + sub % 16, wide, 0.0)
    high = jnp.floor(wide * (1.0 / 256))
    split = jnp.concatenate([high, wide - high * 256.0], axis=1).astype(BF)
    both = sum(dot(pm[q], split[q * BLOCK:(q + 1) * BLOCK]) for q in range(4))
    dpart[...] = both[:, :128] * 256.0 + both[:, 128:]
    c_deg = to_other(dpart.at[other_rows, :], drecv, 3)
    c_deg.start()

    for t in range(4):
        blk = block_of(t)
        wait_block(t, recv_f, fr_sem)
        part = recv_f[rows_at(blk * BLOCK, BLOCK, BLOCK), :]
        if t == 0:
            nsum[...] = dot(pm[blk], part)
        elif t < 3:
            nsum[...] += dot(pm[blk], part)
        else:
            nsum[other_rows, :] += dot(pm[blk, other_rows, :], part)
            c_sum = to_other(nsum.at[other_rows, :], nrecv, 4)
            c_sum.start()
            mine = nsum[own_rows, :] + dot(pm[blk, own_rows, :], part)

    c_deg.wait_recv()
    degree = jnp.sum(dpart[own_rows, :] + drecv[...], axis=1, keepdims=True)
    divisor = jnp.maximum(degree, 1.0)
    c_sum.wait_recv()
    mean = ((mine + nrecv[...]) / divisor).astype(BF)
    pre = pre_self + dot(mean, w_neigh[...])
    gate = jax.nn.sigmoid(pre)
    pre_grad = (up[...].astype(F32) * (gate + pre * gate * (1.0 - gate))).astype(BF)
    mg[own_rows, :] = (dot(pre_grad, w_neigh[...], NT) / divisor).astype(BF)
    c_mg = to_other(mg.at[own_rows, :], mg.at[own_rows, :], 5)
    c_mg.start()
    term[0] = dot(feat[...], pre_grad, TN)
    term[1] = dot(mean, pre_grad, TN)
    c_term = to_other(term.at[o], trecv, 6)
    c_term.start()
    bb[m] = jnp.sum(pre_grad.astype(F32), axis=0, keepdims=True)

    def return_block(t):
        blk = block_of(t)
        here = rows_at(blk * BLOCK, BLOCK, BLOCK)
        gsend[here, :] = dot(pt[blk], mg[...]).astype(BF)
        send_block(t, gsend, recv_b, bs_sem, br_sem, False)

    def spread_to(peers, of, source, target, n):
        def step(k, c):
            pltpu.make_async_remote_copy(
                source(k), target, ar_send.at[n], ar_recv.at[n],
                device_id=(of(k), r), device_id_type=MESH,
            ).start()
            return c

        lax.fori_loop(1, peers, step, 0)

    def plane(k):
        return ((m + k) % 16) * 8 + z

    def line(k):
        return m * 8 + (z + k) % 8

    def wait_all(ref, count, sem):
        part = ref.at[pl.ds(0, count)]
        pltpu.make_async_copy(part, part, sem).wait()

    c_mg.wait_recv()
    return_block(0)
    hidden[...] = (pre * gate).astype(BF)
    selfg[...] = dot(pre_grad, w_self[...], NT)

    c_term.wait_recv()
    tsum = term.at[r]
    tsum[...] += trecv[...]
    spread_to(
        16, plane,
        lambda k: tsum.at[rows_at(((m + k) % 16) * 16, 16, 16), :], rs.at[m], 0,
    )
    spread_to(16, plane, lambda k: bb.at[m], bb.at[m], 1)
    rs[m] = tsum[rows_at(m * 16, 16, 16), :]
    return_block(1)

    wait_all(rs, 15, ar_recv.at[0])
    wait_all(bb, 15, ar_recv.at[1])
    zr[z] = jnp.sum(rs[...], axis=0)
    bz[z] = jnp.sum(bb[...], axis=0)
    spread_to(8, line, lambda k: zr.at[z], zr.at[z], 2)
    spread_to(8, line, lambda k: bz.at[z], bz.at[z], 3)
    return_block(2)

    scale = 1.0 / math.sqrt(131072)
    wait_all(zr, 7, ar_recv.at[2])
    wait_all(bz, 7, ar_recv.at[3])
    ag[r, m] = jnp.sum(zr[...], axis=0) * scale
    b2[r] = jnp.sum(bz[...], axis=0)
    spread_to(16, plane, lambda k: ag.at[r, m], ag.at[r, m], 4)
    c_bias = to_other(b2.at[r], b2.at[r], 7)
    c_bias.start()
    return_block(3)

    wait_all(ag.at[r], 15, ar_recv.at[4])
    c_ag = to_other(ag.at[r], ag.at[r], 8)
    c_ag.start()

    for t in range(4):
        blk = block_of(t)
        wait_block(t, recv_b, br_sem)
        part = recv_b[rows_at(blk * BLOCK, BLOCK, BLOCK), :]
        if t == 0:
            esum[...] = dot(at[blk], part)
        elif t < 3:
            esum[...] += dot(at[blk], part)
        else:
            esum[other_rows, :] += dot(at[blk, other_rows, :], part)
            c_edge = to_other(esum.at[other_rows, :], erecv, 9)
            c_edge.start()
            selfg[...] += esum[own_rows, :] + dot(at[blk, own_rows, :], part)

    c_bias.wait_recv()
    c_ag.wait_recv()
    gself[...] = ag[0].reshape(256, 256)
    gneigh[...] = ag[1].reshape(256, 256)
    gbias[...] = (b2[0] + b2[1]) * scale
    c_edge.wait_recv()
    igrad[...] = (selfg[...] + erecv[...]).astype(BF)

    for copy in (c_src, c_slot, c_feat, c_deg, c_sum, c_mg, c_term, c_bias, c_ag, c_edge):
        copy.wait_send()

    def sent(ref, count, sem):
        part = ref.at[pl.ds(0, count)]
        pltpu.make_async_copy(part, part, sem).wait()

    @pl.when(is_home)
    def _():
        sent(sums, 63 * MSG, fs_sem)
        sent(gsend, 63 * MSG, bs_sem)
        sent(crecv, 63, cs_sem)

    @pl.when(jnp.logical_not(is_home))
    def _():
        sent(sums, 64 * MSG, fs_sem)
        sent(gsend, 64 * MSG, bs_sem)
        sent(crecv, 64, cs_sem)

    sent(rs, 15, ar_send.at[0])
    sent(bb, 15, ar_send.at[1])
    sent(zr, 7, ar_send.at[2])
    sent(bz, 7, ar_send.at[3])
    sent(rs, 15, ar_send.at[4])


def shards(features, w_self, w_neigh, bias_vector, upstream, sources, edge_slots, mirror_rows):
    vmem = pl.BlockSpec(memory_space=pltpu.VMEM)
    scratch = [
        pltpu.VMEM((1, 4096), jnp.int32),
        pltpu.VMEM((1, 4096), jnp.int32),
        pltpu.VMEM((1024, 256), BF),
        pltpu.VMEM((4, 1024, CHUNK), F8),
        pltpu.VMEM((4, 1024, BLOCK), BF),
        pltpu.VMEM((1024, 256), BF),
        pltpu.VMEM((8, 1, 128), F32),
        pltpu.VMEM((1024, 256), BF),
        pltpu.VMEM((64, 1, 128), F32),
        pltpu.VMEM((4, BLOCK, 1024), BF),
        pltpu.VMEM((4, 1024, BLOCK), BF),
        pltpu.VMEM((1024, 256), F32),
        pltpu.VMEM((512, 256), F32),
        pltpu.VMEM((1024, 128), F32),
        pltpu.VMEM((512, 128), F32),
        pltpu.VMEM((1024, 256), BF),
        pltpu.VMEM((1024, 256), BF),
        pltpu.VMEM((1024, 256), BF),
        pltpu.VMEM((1024, 256), F32),
        pltpu.VMEM((512, 256), F32),
        pltpu.VMEM((512, 256), F32),
        pltpu.VMEM((2, 256, 256), F32),
        pltpu.VMEM((256, 256), F32),
        pltpu.VMEM((16, 16, 256), F32),
        pltpu.VMEM((8, 16, 256), F32),
        pltpu.VMEM((2, 16, 16, 256), F32),
        pltpu.VMEM((16, 1, 256), F32),
        pltpu.VMEM((8, 1, 256), F32),
        pltpu.VMEM((2, 1, 256), F32),
        pltpu.SemaphoreType.DMA((10,)),
        pltpu.SemaphoreType.DMA((10,)),
        pltpu.SemaphoreType.DMA,
        pltpu.SemaphoreType.DMA((4,)),
        pltpu.SemaphoreType.DMA,
        pltpu.SemaphoreType.DMA,
        pltpu.SemaphoreType.DMA,
        pltpu.SemaphoreType.DMA((4,)),
        pltpu.SemaphoreType.DMA((5,)),
        pltpu.SemaphoreType.DMA((5,)),
    ]
    hidden, igrad, gself, gneigh, gbias = pl.pallas_call(
        kernel,
        out_shape=(
            jax.ShapeDtypeStruct((512, 256), BF),
            jax.ShapeDtypeStruct((512, 256), BF),
            jax.ShapeDtypeStruct((256, 256), F32),
            jax.ShapeDtypeStruct((256, 256), F32),
            jax.ShapeDtypeStruct((1, 256), F32),
        ),
        in_specs=[vmem] * 8,
        out_specs=(vmem,) * 5,
        scratch_shapes=scratch,
        compiler_params=pltpu.CompilerParams(
            collective_id=0, has_side_effects=True, vmem_limit_bytes=48 * 2**20
        ),
        name="sage_layer",
    )(
        features, w_self, w_neigh, bias_vector.reshape(1, -1), upstream,
        sources.reshape(1, -1), edge_slots.reshape(1, -1), mirror_rows[0],
    )
    return hidden, igrad, gself, gneigh, gbias.reshape(-1)


def solution(mesh):
    in_specs = (
        P(("dom", "rep"), None),
        P(),
        P(),
        P(),
        P(("dom", "rep"), None),
        P(("dom", "rep")),
        P(("dom", "rep")),
        P("dom", None, None),
    )
    out_specs = (P(("dom", "rep"), None), P(("dom", "rep"), None), P(), P(), P())
    return jax.shard_map(shards, mesh=mesh, in_specs=in_specs, out_specs=out_specs, check_vma=False)
```

time: 456 us -> 87.2 us (0.19)
  waiting for transfers between devices: 237 us -> 0 us
  blocking collectives: 86.1 us -> 0 us
  Pallas kernels: 0 us -> 77.7 us
  matrix products: 38.9 us -> 0 us
  local copies, waits for them, and re-layouts: 44.5 us -> 8.55 us
  starting transfers between devices: 26.4 us -> 0 us
  between operations: 14.6 us -> 0.69 us
  other arithmetic: 7.94 us -> 0 us
    psum x1 -> x0, waiting for transfers between devices: 132 us -> none  [shards(): lax.psum((self_term, neigh_term, bias_term), ('dom', 'rep'))]
    all_to_all x3 -> x0, waiting for transfers between devices: 90.2 us -> none  [the longest x1 52.5 us: shards(): lax.all_to_all(slot_sums, 'dom', split_axis=0, concat_axis=0, tiled=True)]
    pallas_call x0 -> x1, Pallas kernels: none -> 77.7 us  [shards(): pl.pallas_call(kernel, out_shape=(jax.ShapeDtypeStruct((512, 256), BF), j...]
    psum x1 -> x0, blocking collectives: 72.9 us -> none  [shards(): lax.psum((self_term, neigh_term, bias_term), ('dom', 'rep'))]
    gather x5 -> x0, local copies, waits for them, and re-layouts: 39 us -> none  [the longest x2 15 us: block_step(): picked = part_rows[source_block]]
    dot_general x12 -> x0, matrix products: 38.9 us -> none  [the longest x4 22.6 us: block_step(): lax.dot_general(selector, picked, dims, preferred_element_type=jnp.float32)]
    all_to_all x3 -> x0, starting transfers between devices: 26.1 us -> none  [the longest x1 13.8 us: shards(): lax.all_to_all(slot_sums, 'dom', split_axis=0, concat_axis=0, tiled=True)]
    reduce_scatter x2 -> x0, waiting for transfers between devices: 14.7 us -> none  [the longest x1 14.7 us: shards(): lax.psum_scatter(edge_grads, 'rep', scatter_dimension=0, tiled=True)]
  transfers between devices with their start and end apart: 6 -> 0, of which waited for: 5 -> 0; matrix products, arithmetic and copies ran while one was open for 8% -> 0% of each run, Pallas kernels for 0% -> 0%
where the time goes in v1:
time: 87.2 us; the launch traced here: 87 us
  Pallas kernels  77.7 us (89%)
  local copies, waits for them, and re-layouts  8.55 us (10%)
    pallas_call x1, Pallas kernels, shards(): pl.pallas_call(kernel, out_shape=(jax.ShapeDtypeStruct((512, 256), BF), j...  77.7 us
    unnamed x20, local copies, waits for them, and re-layouts  8.55 us

profile of v1, /device:TPU:1, one launch (start us, length us, event | category | flops | bytes accessed | tf_op | source)
XLA Modules:
  0.0 87.0 jit_solution(13094340049317598164)
XLA Ops:
  0.6 0.0 copy-start.4
  0.6 0.0 copy-start.5
  0.7 0.8 copy.13
  1.5 0.0 copy-start.6
  1.5 0.0 copy-done.4
  1.5 0.0 copy-done.5
  1.5 0.7 copy-done.6
  2.1 0.0 copy-start
  2.1 0.9 %copy-done = bf16[512,256]{1,0:T(8,128)(2,1)S(1)} copy-done((bf16[512,256]{1,0:T(8,128)(2,1)S(1)}, bf16[512,256]{1,0:T(8,128)(2,1)}, u32[]{:S(2)}) %copy-start) | copy-done | bytes 262168
  3.1 0.0 copy-start.1
  3.1 0.9 %copy-done.1 = bf16[512,256]{1,0:T(8,128)(2,1)S(1)} copy-done((bf16[512,256]{1,0:T(8,128)(2,1)S(1)}, bf16[512,256]{1,0:T(8,128)(2,1)}, u32[]{:S(2)}) %copy-start.1) | copy-done | bytes 262168
  4.0 0.0 copy-start.2
  4.0 0.9 %copy-done.2 = bf16[256,256]{1,0:T(8,128)(2,1)S(1)} copy-done((bf16[256,256]{1,0:T(8,128)(2,1)S(1)}, bf16[256,256]{1,0:T(8,128)(2,1)}, u32[]{:S(2)}) %copy-start.2) | copy-done | bytes 131096
  4.9 0.0 copy-start.3
  4.9 0.9 %copy-done.3 = bf16[256,256]{1,0:T(8,128)(2,1)S(1)} copy-done((bf16[256,256]{1,0:T(8,128)(2,1)S(1)}, bf16[256,256]{1,0:T(8,128)(2,1)}, u32[]{:S(2)}) %copy-start.3) | copy-done | bytes 131096
  5.9 77.7 %sage_layer.1 = (bf16[512,256]{1,0:T(8,128)(2,1)S(1)}, bf16[512,256]{1,0:T(8,128)(2,1)S(1)}, f32[256,256]{1,0:T(8,128)S(1)}, f32[256,256]{1,0:T(8,128)S(1)}, f32[1,256]{1,0:T(1,128)S(1)}) custom-call(bf16[512,256]{1,0:T(8,128)(2,1)S(1)} %copy-done, bf16[256,256]{1,0:T(8,128)(2,1)S(1)} %copy-done.2, bf16[256,256]{1,0:T(8,128)(2,1)S(1)} %copy-done.3, ...), custom_call_target="tpu_custom_call" | custom-call | tf_op jit(solution)/shard_map/sage_layer/pallas_call | solution.py:375
  83.6 0.7 copy.19
  84.3 0.7 copy.20
  85.0 0.7 copy.21
  85.7 0.7 copy.22
  86.4 0.6 copy.23
Async XLA Ops:
  0.6 0.8 copy-start.4
  0.6 0.8 copy-start.5
  1.5 0.7 copy-start.6
  2.1 0.9 %copy-start = (bf16[512,256]{1,0:T(8,128)(2,1)S(1)}, bf16[512,256]{1,0:T(8,128)(2,1)}, u32[]{:S(2)}) copy-start(bf16[512,256]{1,0:T(8,128)(2,1)} %feat.1) | copy-start | bytes 786436
  3.1 0.9 %copy-start.1 = (bf16[512,256]{1,0:T(8,128)(2,1)S(1)}, bf16[512,256]{1,0:T(8,128)(2,1)}, u32[]{:S(2)}) copy-start(bf16[512,256]{1,0:T(8,128)(2,1)} %up.1) | copy-start | bytes 786436
  4.0 0.9 %copy-start.2 = (bf16[256,256]{1,0:T(8,128)(2,1)S(1)}, bf16[256,256]{1,0:T(8,128)(2,1)}, u32[]{:S(2)}) copy-start(bf16[256,256]{1,0:T(8,128)(2,1)} %w_self.1) | copy-start | bytes 393220
  4.9 0.9 %copy-start.3 = (bf16[256,256]{1,0:T(8,128)(2,1)S(1)}, bf16[256,256]{1,0:T(8,128)(2,1)}, u32[]{:S(2)}) copy-start(bf16[256,256]{1,0:T(8,128)(2,1)} %w_neigh.1) | copy-start | bytes 393220

commit v2 on v1

v2 whole, which is shorter than its diff:
```python
import functools
import math

import jax
import jax.numpy as jnp
from jax import lax
from jax.experimental import pallas as pl
from jax.experimental.pallas import tpu as pltpu
from jax.sharding import PartitionSpec as P

MESH = pl.DeviceIdType.MESH
BF = jnp.bfloat16
F32 = jnp.float32
F8 = jnp.float8_e4m3fn

NN = (((1,), (0,)), ((), ()))
NT = (((1,), (1,)), ((), ()))
TN = (((0,), (0,)), ((), ()))

CHUNK = 2048
BLOCK = 256
MSG = 16


def dot(a, b, dims=NN):
    return lax.dot_general(a, b, dims, preferred_element_type=F32)


def one_hot_cols(index_row, count, dtype):
    n = index_row.shape[1]
    rows = lax.broadcasted_iota(jnp.int32, (count, n), 0).astype(jnp.int16)
    wanted = jnp.broadcast_to(index_row, (count, n)).astype(jnp.int16)
    return jnp.where(rows == wanted, jnp.ones((), BF), jnp.zeros((), BF)).astype(dtype)


def rows_at(start, count, unit):
    return pl.ds(pl.multiple_of(start, unit), count)


def kernel(
    feat_h, w_self_h, w_neigh_h, bias_h, up_h, src_h, slot_h, mir_h,
    hidden, igrad, gself, gneigh, gbias,
    w_self, w_neigh, bias, up, src, slot, mir, mcol, col_ref,
    fall, ssrc, at, sums, cnt, recv_f, crecv,
    pt, pm, nsum, nrecv, dpart, drecv, mg, gsend, recv_b, esum, erecv, presf, mn, pg,
    term, trecv, rs, zr, ag, bb, bz, b2,
    in_sem, rep_send, rep_recv, fs_sem, fr_sem, cs_sem, cr_sem, bs_sem, br_sem,
    ar_send, ar_recv,
):
    p = lax.axis_index("dom")
    r = lax.axis_index("rep")
    o = 1 - r
    x, y, z = p // 32, (p // 8) % 4, p % 8
    h, a, b = x // 2, x % 2, y // 2
    m = x * 4 + y
    my_idx = (a * 4 + y) * 8 + z
    is_home = h == r
    own_rows = rows_at(r * 512, 512, 512)
    other_rows = rows_at(o * 512, 512, 512)

    bar = pltpu.get_barrier_semaphore()

    def tell(dom, rep):
        pl.semaphore_signal(bar, inc=1, device_id=(dom, rep), device_id_type=MESH)

    loads = [
        pltpu.make_async_copy(source, target, in_sem.at[n])
        for n, (source, target) in enumerate((
            (src_h, src.at[0]), (slot_h, slot.at[0]), (feat_h, fall.at[own_rows, :]),
            (mir_h, mir), (w_self_h, w_self), (bias_h, bias), (w_neigh_h, w_neigh), (up_h, up),
        ))
    ]
    for load in loads:
        load.start()

    tell(p, o)

    def tell_half(k, c):
        @pl.when(jnp.logical_not(jnp.logical_and(is_home, k == my_idx)))
        def _():
            tell(r * 64 + k, h)

        return c

    lax.fori_loop(0, 64, tell_half, 0)
    lax.fori_loop(1, 16, lambda k, c: (tell(((m + k) % 16) * 8 + z, r), c)[1], 0)
    lax.fori_loop(1, 8, lambda k, c: (tell(m * 8 + (z + k) % 8, r), c)[1], 0)

    def pick_sources(which):
        def step(c, carry):
            cols = rows_at(c * CHUNK, CHUNK, CHUNK)
            ssrc[which * 2 + c] = one_hot_cols(src[which, :, cols], 1024, F8)
            return carry

        lax.fori_loop(0, 2, step, 0)

    loads[0].wait()
    pick_sources(0)
    for load in loads[1:3]:
        load.wait()

    pl.semaphore_wait(bar, 87 - jnp.where(is_home, 1, 0))

    def to_other(source, target, n):
        return pltpu.make_async_remote_copy(
            source, target, rep_send.at[n], rep_recv.at[n],
            device_id=(p, o), device_id_type=MESH,
        )

    c_src = to_other(src.at[0], src.at[1], 0)
    c_slot = to_other(slot.at[0], slot.at[1], 1)
    c_feat = to_other(fall.at[own_rows, :], fall.at[own_rows, :], 2)
    c_src.start()
    c_slot.start()
    c_feat.start()
    c_src.wait_recv()
    pick_sources(1)
    c_slot.wait_recv()
    c_feat.wait_recv()

    def send_block(t, source, target, send_sem, recv_sem, counts):
        i, j = (a + t // 2) % 2, (b + t % 2) % 2

        def step(k, c):
            line = i * 4 + 2 * j + k // 8
            idx = line * 8 + (z + k) % 8
            here = rows_at(idx * MSG, MSG, MSG)
            there = rows_at(my_idx * MSG, MSG, MSG)
            is_self = jnp.logical_and(is_home, idx == my_idx)

            @pl.when(jnp.logical_not(is_self))
            def _():
                dev = (r * 64 + idx, h)
                if counts:
                    pltpu.make_async_remote_copy(
                        cnt.at[line], crecv.at[my_idx], cs_sem, cr_sem,
                        device_id=dev, device_id_type=MESH,
                    ).start()
                pltpu.make_async_remote_copy(
                    source.at[here, :], target.at[there, :], send_sem, recv_sem.at[t],
                    device_id=dev, device_id_type=MESH,
                ).start()

            @pl.when(is_self)
            def _():
                if counts:
                    pltpu.make_async_copy(cnt.at[line], crecv.at[my_idx], cr_sem).start()
                pltpu.make_async_copy(
                    source.at[here, :], target.at[there, :], recv_sem.at[t]
                ).start()

            return c

        lax.fori_loop(0, 16, step, 0)

    def block_of(t):
        return (a + t // 2) % 2 * 2 + (b + t % 2) % 2

    def wait_block(t, target, recv_sem):
        part = target.at[rows_at(block_of(t) * BLOCK, BLOCK, BLOCK), :]
        pltpu.make_async_copy(part, part, recv_sem.at[t]).wait()

    def count_block(t, carry):
        blk = block_of(t)
        base = r * 1024 + blk * BLOCK
        acc = None
        for c in range(4):
            lo = (c % 2) * CHUNK
            sel = one_hot_cols(slot[c // 2, :, lo:lo + CHUNK] - base, BLOCK, F8)
            d = dot(ssrc[c], sel, NT)
            acc = d if acc is None else acc + d
        counted = jnp.sum(acc, axis=0, keepdims=True)
        cnt[blk * 2] = counted[:, :128]
        cnt[blk * 2 + 1] = counted[:, 128:]
        table = acc.astype(BF)
        at[blk] = table
        sums[rows_at(blk * BLOCK, BLOCK, BLOCK), :] = dot(table, fall[...], TN).astype(BF)
        send_block(t, sums, recv_f, fs_sem, fr_sem, True)
        return carry

    lax.fori_loop(0, 4, count_block, 0)

    for load in loads[3:]:
        load.wait()

    mcol[...] = jnp.concatenate([mir[...].astype(F32)] * 8, axis=0).T
    spread = mcol[rows_at(r * 64, 64, 64), :]
    spread = jnp.broadcast_to(spread[:, None, :], (64, 16, 128)).reshape(1024, 128)
    lane = lax.broadcasted_iota(jnp.int32, (1024, 128), 1)
    sub = lax.broadcasted_iota(jnp.int32, (1024, 128), 0)
    col = jnp.sum(jnp.where(lane == sub % 16, spread, 0.0), axis=1, keepdims=True)
    col_ref[...] = jnp.broadcast_to(col, (1024, 128)).reshape(4, BLOCK, 128)

    def master_block(q, carry):
        part = col_ref[q]
        pm[q] = one_hot_cols(part.T[0:1].astype(jnp.int32), 1024, BF)
        pt[q] = pm[q].T
        return carry

    lax.fori_loop(0, 4, master_block, 0)

    nsum[...] = jnp.zeros_like(nsum)
    presf[...] = dot(fall[own_rows, :], w_self[...]) + bias[...]

    pltpu.make_async_copy(crecv, crecv, cr_sem).wait()
    got = crecv[...].reshape(64, 128)
    wide = jnp.broadcast_to(got[:, None, :], (64, 16, 128)).reshape(1024, 128)
    wide = jnp.where(lane == z * 16 + sub % 16, wide, 0.0)
    high = jnp.floor(wide * (1.0 / 256))
    split = jnp.concatenate([high, wide - high * 256.0], axis=1).astype(BF)
    both = sum(dot(pm[q], split[q * BLOCK:(q + 1) * BLOCK]) for q in range(4))
    dpart[...] = both[:, :128] * 256.0 + both[:, 128:]
    c_deg = to_other(dpart.at[other_rows, :], drecv, 3)
    c_deg.start()

    c_sum = to_other(nsum.at[other_rows, :], nrecv, 4)

    def place_block(t, carry):
        blk = block_of(t)
        wait_block(t, recv_f, fr_sem)
        part = recv_f[rows_at(blk * BLOCK, BLOCK, BLOCK), :]
        nsum[other_rows, :] += dot(pm[blk, other_rows, :], part)

        @pl.when(t == 3)
        def _():
            c_sum.start()

        nsum[own_rows, :] += dot(pm[blk, own_rows, :], part)
        return carry

    lax.fori_loop(0, 4, place_block, 0)

    c_deg.wait_recv()
    c_sum.wait_recv()

    def dense_block(q, carry):
        rows = rows_at(q * 128, 128, 128)
        mine = rows_at(r * 512 + q * 128, 128, 128)
        degree = jnp.sum(dpart[mine, :] + drecv[rows, :], axis=1, keepdims=True)
        divisor = jnp.maximum(degree, 1.0)
        mean = ((nsum[mine, :] + nrecv[rows, :]) / divisor).astype(BF)
        pre = presf[rows, :] + dot(mean, w_neigh[...])
        gate = jax.nn.sigmoid(pre)
        pre_grad = up[rows, :].astype(F32) * (gate + pre * gate * (1.0 - gate))
        pre_grad = pre_grad.astype(BF)
        mg[mine, :] = (dot(pre_grad, w_neigh[...], NT) / divisor).astype(BF)
        hidden[rows, :] = (pre * gate).astype(BF)
        mn[rows, :] = mean
        pg[rows, :] = pre_grad
        return carry

    lax.fori_loop(0, 4, dense_block, 0)
    c_mg = to_other(mg.at[own_rows, :], mg.at[own_rows, :], 5)
    c_mg.start()
    term[0] = dot(fall[own_rows, :], pg[...], TN)
    term[1] = dot(mn[...], pg[...], TN)
    c_term = to_other(term.at[o], trecv, 6)
    c_term.start()
    bb[m] = jnp.sum(pg[...].astype(F32), axis=0, keepdims=True)

    def spread_to(peers, of, source, target, n):
        def step(k, c):
            pltpu.make_async_remote_copy(
                source(k), target, ar_send.at[n], ar_recv.at[n],
                device_id=(of(k), r), device_id_type=MESH,
            ).start()
            return c

        lax.fori_loop(1, peers, step, 0)

    def plane(k):
        return ((m + k) % 16) * 8 + z

    def line(k):
        return m * 8 + (z + k) % 8

    def wait_all(ref, count, sem):
        part = ref.at[pl.ds(0, count)]
        pltpu.make_async_copy(part, part, sem).wait()

    scale = 1.0 / math.sqrt(131072)
    tsum = term.at[r]
    c_bias = to_other(b2.at[r], b2.at[r], 7)
    c_ag = to_other(ag.at[r], ag.at[r], 8)

    def reduce_plane():
        c_term.wait_recv()
        tsum[...] += trecv[...]
        spread_to(
            16, plane,
            lambda k: tsum.at[rows_at(((m + k) % 16) * 16, 16, 16), :], rs.at[m], 0,
        )
        spread_to(16, plane, lambda k: bb.at[m], bb.at[m], 1)
        rs[m] = tsum[rows_at(m * 16, 16, 16), :]

    def reduce_line():
        wait_all(rs, 15, ar_recv.at[0])
        wait_all(bb, 15, ar_recv.at[1])
        zr[z] = jnp.sum(rs[...], axis=0)
        bz[z] = jnp.sum(bb[...], axis=0)
        spread_to(8, line, lambda k: zr.at[z], zr.at[z], 2)
        spread_to(8, line, lambda k: bz.at[z], bz.at[z], 3)

    def gather_plane():
        wait_all(zr, 7, ar_recv.at[2])
        wait_all(bz, 7, ar_recv.at[3])
        ag[r, m] = jnp.sum(zr[...], axis=0) * scale
        b2[r] = jnp.sum(bz[...], axis=0)
        spread_to(16, plane, lambda k: ag.at[r, m], ag.at[r, m], 4)
        c_bias.start()

    def gather_cores():
        wait_all(ag.at[r], 15, ar_recv.at[4])
        c_ag.start()

    c_mg.wait_recv()

    def return_block(t, carry):
        blk = block_of(t)
        here = rows_at(blk * BLOCK, BLOCK, BLOCK)
        gsend[here, :] = dot(pt[blk], mg[...]).astype(BF)
        send_block(t, gsend, recv_b, bs_sem, br_sem, False)

        @pl.when(t == 0)
        def _():
            reduce_plane()

        return carry

    lax.fori_loop(0, 4, return_block, 0)

    esum[own_rows, :] = dot(pg[...], w_self[...], NT)
    esum[other_rows, :] = jnp.zeros((512, 256), F32)
    c_edge = to_other(esum.at[other_rows, :], erecv, 9)

    def edge_block(t, carry):
        blk = block_of(t)

        @pl.when(t == 0)
        def _():
            reduce_line()

        @pl.when(t == 1)
        def _():
            gather_plane()

        @pl.when(t == 3)
        def _():
            gather_cores()

        wait_block(t, recv_b, br_sem)
        part = recv_b[rows_at(blk * BLOCK, BLOCK, BLOCK), :]
        esum[other_rows, :] += dot(at[blk, other_rows, :], part)

        @pl.when(t == 3)
        def _():
            c_edge.start()

        esum[own_rows, :] += dot(at[blk, own_rows, :], part)
        return carry

    lax.fori_loop(0, 4, edge_block, 0)

    c_bias.wait_recv()
    c_ag.wait_recv()
    gself[...] = ag[0].reshape(256, 256)
    gneigh[...] = ag[1].reshape(256, 256)
    gbias[...] = (b2[0] + b2[1]) * scale
    c_edge.wait_recv()
    igrad[...] = (esum[own_rows, :] + erecv[...]).astype(BF)

    for copy in (c_src, c_slot, c_feat, c_deg, c_sum, c_mg, c_term, c_bias, c_ag, c_edge):
        copy.wait_send()

    def sent(ref, count, sem):
        part = ref.at[pl.ds(0, count)]
        pltpu.make_async_copy(part, part, sem).wait()

    @pl.when(is_home)
    def _():
        sent(sums, 63 * MSG, fs_sem)
        sent(gsend, 63 * MSG, bs_sem)
        sent(crecv, 63, cs_sem)

    @pl.when(jnp.logical_not(is_home))
    def _():
        sent(sums, 64 * MSG, fs_sem)
        sent(gsend, 64 * MSG, bs_sem)
        sent(crecv, 64, cs_sem)

    sent(rs, 15, ar_send.at[0])
    sent(bb, 15, ar_send.at[1])
    sent(zr, 7, ar_send.at[2])
    sent(bz, 7, ar_send.at[3])
    sent(rs, 15, ar_send.at[4])


def write_out(*refs):
    n = len(refs) // 2
    sems = refs[-1]
    copies = [pltpu.make_async_copy(refs[i], refs[n + i], sems.at[i]) for i in range(n)]
    for copy in copies:
        copy.start()
    for copy in copies:
        copy.wait()


def shards(features, w_self, w_neigh, bias_vector, upstream, sources, edge_slots, mirror_rows):
    vmem = pl.BlockSpec(memory_space=pltpu.VMEM)
    hbm = pl.BlockSpec(memory_space=pltpu.HBM)
    scratch = [
        pltpu.VMEM((256, 256), BF),
        pltpu.VMEM((256, 256), BF),
        pltpu.VMEM((1, 256), F32),
        pltpu.VMEM((512, 256), BF),
        pltpu.VMEM((2, 1, 4096), jnp.int32),
        pltpu.VMEM((2, 1, 4096), jnp.int32),
        pltpu.VMEM((16, 128), jnp.int32),
        pltpu.VMEM((128, 128), F32),
        pltpu.VMEM((4, BLOCK, 128), F32),
        pltpu.VMEM((1024, 256), BF),
        pltpu.VMEM((4, 1024, CHUNK), F8),
        pltpu.VMEM((4, 1024, BLOCK), BF),
        pltpu.VMEM((1024, 256), BF),
        pltpu.VMEM((8, 1, 128), F32),
        pltpu.VMEM((1024, 256), BF),
        pltpu.VMEM((64, 1, 128), F32),
        pltpu.VMEM((4, BLOCK, 1024), BF),
        pltpu.VMEM((4, 1024, BLOCK), BF),
        pltpu.VMEM((1024, 256), F32),
        pltpu.VMEM((512, 256), F32),
        pltpu.VMEM((1024, 128), F32),
        pltpu.VMEM((512, 128), F32),
        pltpu.VMEM((1024, 256), BF),
        pltpu.VMEM((1024, 256), BF),
        pltpu.VMEM((1024, 256), BF),
        pltpu.VMEM((1024, 256), F32),
        pltpu.VMEM((512, 256), F32),
        pltpu.VMEM((512, 256), F32),
        pltpu.VMEM((512, 256), BF),
        pltpu.VMEM((512, 256), BF),
        pltpu.VMEM((2, 256, 256), F32),
        pltpu.VMEM((256, 256), F32),
        pltpu.VMEM((16, 16, 256), F32),
        pltpu.VMEM((8, 16, 256), F32),
        pltpu.VMEM((2, 16, 16, 256), F32),
        pltpu.VMEM((16, 1, 256), F32),
        pltpu.VMEM((8, 1, 256), F32),
        pltpu.VMEM((2, 1, 256), F32),
        pltpu.SemaphoreType.DMA((8,)),
        pltpu.SemaphoreType.DMA((10,)),
        pltpu.SemaphoreType.DMA((10,)),
        pltpu.SemaphoreType.DMA,
        pltpu.SemaphoreType.DMA((4,)),
        pltpu.SemaphoreType.DMA,
        pltpu.SemaphoreType.DMA,
        pltpu.SemaphoreType.DMA,
        pltpu.SemaphoreType.DMA((4,)),
        pltpu.SemaphoreType.DMA((5,)),
        pltpu.SemaphoreType.DMA((5,)),
    ]
    shapes = (
        jax.ShapeDtypeStruct((512, 256), BF),
        jax.ShapeDtypeStruct((512, 256), BF),
        jax.ShapeDtypeStruct((256, 256), F32),
        jax.ShapeDtypeStruct((256, 256), F32),
        jax.ShapeDtypeStruct((1, 256), F32),
    )
    results = pl.pallas_call(
        kernel,
        out_shape=shapes,
        in_specs=[hbm] * 8,
        out_specs=(vmem,) * 5,
        scratch_shapes=scratch,
        compiler_params=pltpu.CompilerParams(
            collective_id=0, has_side_effects=True, vmem_limit_bytes=63 * 2**20
        ),
        name="sage_layer",
    )(
        features, w_self, w_neigh, bias_vector.reshape(1, -1), upstream,
        sources.reshape(1, -1), edge_slots.reshape(1, -1), jnp.swapaxes(mirror_rows[0], 0, 1),
    )
    hidden, igrad, gself, gneigh, gbias = pl.pallas_call(
        write_out,
        out_shape=shapes,
        in_specs=[vmem] * 5,
        out_specs=(hbm,) * 5,
        scratch_shapes=[pltpu.SemaphoreType.DMA((5,))],
        name="write_out",
    )(*results)
    return hidden, igrad, gself, gneigh, gbias.reshape(-1)


def solution(mesh):
    in_specs = (
        P(("dom", "rep"), None),
        P(),
        P(),
        P(),
        P(("dom", "rep"), None),
        P(("dom", "rep")),
        P(("dom", "rep")),
        P("dom", None, None),
    )
    out_specs = (P(("dom", "rep"), None), P(("dom", "rep"), None), P(), P(), P())
    return jax.shard_map(shards, mesh=mesh, in_specs=in_specs, out_specs=out_specs, check_vma=False)
```

time: 87.2 us -> 72.4 us (0.83)
  local copies, waits for them, and re-layouts: 8.55 us -> 0 us
  Pallas kernels: 77.7 us -> 71.6 us
    unnamed x20 -> x0, local copies, waits for them, and re-layouts: 8.55 us -> none
    pallas_call x1 -> x2, Pallas kernels: 77.7 us -> 71.6 us  [the longest x1 69.4 us: shards(): pl.pallas_call(kernel, out_shape=shapes, in_specs=[hbm] * 8, out_specs=(v...]
where the time goes in v2:
time: 72.4 us; the launch traced here: 72.3 us
  Pallas kernels  71.6 us (99%)
    pallas_call x1, Pallas kernels, shards(): pl.pallas_call(kernel, out_shape=shapes, in_specs=[hbm] * 8, out_specs=(v...  69.4 us
    pallas_call x1, Pallas kernels, shards(): pl.pallas_call(write_out, out_shape=shapes, in_specs=[vmem] * 5, out_spec...  2.2 us

profile of v2, /device:TPU:1, one launch (start us, length us, event | category | flops | bytes accessed | tf_op | source)
XLA Modules:
  0.0 72.3 jit_solution(4837538377177915462)
XLA Ops:
  0.6 69.4 %sage_layer.1 = (bf16[512,256]{1,0:T(8,128)(2,1)}, bf16[512,256]{1,0:T(8,128)(2,1)}, f32[256,256]{1,0:T(8,128)}, f32[256,256]{1,0:T(8,128)}, f32[1,256]{1,0:T(1,128)}) custom-call(bf16[512,256]{1,0:T(8,128)(2,1)} %feat_h.1, bf16[256,256]{1,0:T(8,128)(2,1)} %w_self_h.1, bf16[256,256]{1,0:T(8,128)(2,1)} %w_neigh_h.1, f32[1,256]{1,0:T(1,128)} %bitcast.10, ...), custom_call_target="tpu_custom_call" | custom-call | tf_op jit(solution)/shard_map/sage_layer/pallas_call | solution.py:469
  70.1 2.2 %write_out.1 = (bf16[512,256]{1,0:T(8,128)(2,1)}, bf16[512,256]{1,0:T(8,128)(2,1)}, f32[256,256]{1,0:T(8,128)}, f32[256,256]{1,0:T(8,128)}, f32[1,256]{1,0:T(1,128)}) custom-call(bf16[512,256]{1,0:T(8,128)(2,1)} %get-tuple-element.15.refs_0_, bf16[512,256]{1,0:T(8,128)(2,1)} %get-tuple-element.16.refs_1_, f32[256,256]{1,0:T(8,128)} %get-tuple-element.17.refs_2_, ...), custom_call_target="tpu_custom_call" | custom-call | tf_op jit(solution)/shard_map/write_out/pallas_call | solution.py:483

commit v3 on v2

--- a/solution.py
+++ b/solution.py
@@ -20,6 +20,10 @@
 CHUNK = 2048
 BLOCK = 256
 MSG = 16
+RT = BF
+GT = BF
+CT = BF
+AT = (0, 1, 2, 6)
 
 
 def dot(a, b, dims=NN):
@@ -39,12 +43,13 @@
 
 def kernel(
     feat_h, w_self_h, w_neigh_h, bias_h, up_h, src_h, slot_h, mir_h,
+    hidden_h, igrad_h, gself_h, gneigh_h, gbias_h,
     hidden, igrad, gself, gneigh, gbias,
     w_self, w_neigh, bias, up, src, slot, mir, mcol, col_ref,
     fall, ssrc, at, sums, cnt, recv_f, crecv,
-    pt, pm, nsum, nrecv, dpart, drecv, mg, gsend, recv_b, esum, erecv, presf, mn, pg,
-    term, trecv, rs, zr, ag, bb, bz, b2,
-    in_sem, rep_send, rep_recv, fs_sem, fr_sem, cs_sem, cr_sem, bs_sem, br_sem,
+    pt, pm, nsum, nsend, nrecv, dacc, dpart, drecv, mg, gsend, recv_b, esum, esend, erecv, presf, mn, pg,
+    term, trecv, tsum, rs, zr, ag, bb, bz, b2,
+    in_sem, out_sem, rep_send, rep_recv, fs_sem, fr_sem, cs_sem, cr_sem, bs_sem, br_sem,
     ar_send, ar_recv,
 ):
     p = lax.axis_index("dom")
@@ -72,6 +77,12 @@
     ]
     for load in loads:
         load.start()
+    stores = [
+        pltpu.make_async_copy(source, target, out_sem.at[n])
+        for n, (source, target) in enumerate((
+            (hidden, hidden_h), (igrad, igrad_h), (gself, gself_h), (gneigh, gneigh_h), (gbias, gbias_h),
+        ))
+    ]
 
     tell(p, o)
 
@@ -133,7 +144,7 @@
                 dev = (r * 64 + idx, h)
                 if counts:
                     pltpu.make_async_remote_copy(
-                        cnt.at[line], crecv.at[my_idx], cs_sem, cr_sem,
+                        cnt.at[line], crecv.at[my_idx], cs_sem, cr_sem.at[t],
                         device_id=dev, device_id_type=MESH,
                     ).start()
                 pltpu.make_async_remote_copy(
@@ -144,7 +155,7 @@
             @pl.when(is_self)
             def _():
                 if counts:
-                    pltpu.make_async_copy(cnt.at[line], crecv.at[my_idx], cr_sem).start()
+                    pltpu.make_async_copy(cnt.at[line], crecv.at[my_idx], cr_sem.at[t]).start()
                 pltpu.make_async_copy(
                     source.at[here, :], target.at[there, :], recv_sem.at[t]
                 ).start()
@@ -202,33 +213,44 @@
     nsum[...] = jnp.zeros_like(nsum)
     presf[...] = dot(fall[own_rows, :], w_self[...]) + bias[...]
 
-    pltpu.make_async_copy(crecv, crecv, cr_sem).wait()
-    got = crecv[...].reshape(64, 128)
-    wide = jnp.broadcast_to(got[:, None, :], (64, 16, 128)).reshape(1024, 128)
-    wide = jnp.where(lane == z * 16 + sub % 16, wide, 0.0)
-    high = jnp.floor(wide * (1.0 / 256))
-    split = jnp.concatenate([high, wide - high * 256.0], axis=1).astype(BF)
-    both = sum(dot(pm[q], split[q * BLOCK:(q + 1) * BLOCK]) for q in range(4))
-    dpart[...] = both[:, :128] * 256.0 + both[:, 128:]
-    c_deg = to_other(dpart.at[other_rows, :], drecv, 3)
-    c_deg.start()
-
-    c_sum = to_other(nsum.at[other_rows, :], nrecv, 4)
+    dacc[...] = jnp.zeros_like(dacc)
+
+    c_sum = to_other(nsend, nrecv, 4)
+    c_deg = to_other(dpart, drecv, 3)
 
     def place_block(t, carry):
         blk = block_of(t)
+        places = pl.ds(pl.multiple_of(blk * 16, 16), 16)
+        pltpu.make_async_copy(crecv.at[places], crecv.at[places], cr_sem.at[t]).wait()
+        got = crecv[places].reshape(16, 128)
+        wide = jnp.broadcast_to(got[:, None, :], (16, 16, 128)).reshape(BLOCK, 128)
+        lane = lax.broadcasted_iota(jnp.int32, (BLOCK, 128), 1)
+        sub = lax.broadcasted_iota(jnp.int32, (BLOCK, 128), 0)
+        wide = jnp.where(lane == z * 16 + sub % 16, wide, 0.0)
+        high = jnp.floor(wide * (1.0 / 256))
+        split = jnp.concatenate([high, wide - high * 256.0], axis=1).astype(BF)
+        dacc[other_rows, :] += dot(pm[blk, other_rows, :], split)
+        dacc[own_rows, :] += dot(pm[blk, own_rows, :], split)
+
+        @pl.when(t == 3)
+        def _():
+            dpart[...] = dacc[other_rows, :128] * 256.0 + dacc[other_rows, 128:]
+            c_deg.start()
+
         wait_block(t, recv_f, fr_sem)
         part = recv_f[rows_at(blk * BLOCK, BLOCK, BLOCK), :]
         nsum[other_rows, :] += dot(pm[blk, other_rows, :], part)
 
         @pl.when(t == 3)
         def _():
+            nsend[...] = nsum[other_rows, :].astype(CT)
             c_sum.start()
 
         nsum[own_rows, :] += dot(pm[blk, own_rows, :], part)
         return carry
 
     lax.fori_loop(0, 4, place_block, 0)
+    dacc[own_rows, :128] = dacc[own_rows, :128] * 256.0 + dacc[own_rows, 128:]
 
     c_deg.wait_recv()
     c_sum.wait_recv()
@@ -236,7 +258,7 @@
     def dense_block(q, carry):
         rows = rows_at(q * 128, 128, 128)
         mine = rows_at(r * 512 + q * 128, 128, 128)
-        degree = jnp.sum(dpart[mine, :] + drecv[rows, :], axis=1, keepdims=True)
+        degree = jnp.sum(dacc[mine, :128] + drecv[rows, :], axis=1, keepdims=True)
         divisor = jnp.maximum(degree, 1.0)
         mean = ((nsum[mine, :] + nrecv[rows, :]) / divisor).astype(BF)
         pre = presf[rows, :] + dot(mean, w_neigh[...])
@@ -250,6 +272,7 @@
         return carry
 
     lax.fori_loop(0, 4, dense_block, 0)
+    stores[0].start()
     c_mg = to_other(mg.at[own_rows, :], mg.at[own_rows, :], 5)
     c_mg.start()
     term[0] = dot(fall[own_rows, :], pg[...], TN)
@@ -279,13 +302,12 @@
         pltpu.make_async_copy(part, part, sem).wait()
 
     scale = 1.0 / math.sqrt(131072)
-    tsum = term.at[r]
     c_bias = to_other(b2.at[r], b2.at[r], 7)
     c_ag = to_other(ag.at[r], ag.at[r], 8)
 
     def reduce_plane():
         c_term.wait_recv()
-        tsum[...] += trecv[...]
+        tsum[...] = (term[r] + trecv[...]).astype(RT)
         spread_to(
             16, plane,
             lambda k: tsum.at[rows_at(((m + k) % 16) * 16, 16, 16), :], rs.at[m], 0,
@@ -296,7 +318,7 @@
     def reduce_line():
         wait_all(rs, 15, ar_recv.at[0])
         wait_all(bb, 15, ar_recv.at[1])
-        zr[z] = jnp.sum(rs[...], axis=0)
+        zr[z] = jnp.sum(rs[...].astype(F32), axis=0).astype(RT)
         bz[z] = jnp.sum(bb[...], axis=0)
         spread_to(8, line, lambda k: zr.at[z], zr.at[z], 2)
         spread_to(8, line, lambda k: bz.at[z], bz.at[z], 3)
@@ -304,7 +326,7 @@
     def gather_plane():
         wait_all(zr, 7, ar_recv.at[2])
         wait_all(bz, 7, ar_recv.at[3])
-        ag[r, m] = jnp.sum(zr[...], axis=0) * scale
+        ag[r, m] = (jnp.sum(zr[...].astype(F32), axis=0) * scale).astype(GT)
         b2[r] = jnp.sum(bz[...], axis=0)
         spread_to(16, plane, lambda k: ag.at[r, m], ag.at[r, m], 4)
         c_bias.start()
@@ -312,6 +334,13 @@
     def gather_cores():
         wait_all(ag.at[r], 15, ar_recv.at[4])
         c_ag.start()
+
+    stages = (reduce_plane, reduce_line, gather_plane, gather_cores)
+
+    def stages_at(t, first):
+        for stage, when in zip(stages, AT):
+            if first <= when < first + 4:
+                pl.when(t == when - first)(stage)
 
     c_mg.wait_recv()
 
@@ -320,40 +349,28 @@
         here = rows_at(blk * BLOCK, BLOCK, BLOCK)
         gsend[here, :] = dot(pt[blk], mg[...]).astype(BF)
         send_block(t, gsend, recv_b, bs_sem, br_sem, False)
-
-        @pl.when(t == 0)
-        def _():
-            reduce_plane()
-
+        stages_at(t, 0)
         return carry
 
+    if AT[0] < 0:
+        reduce_plane()
     lax.fori_loop(0, 4, return_block, 0)
 
     esum[own_rows, :] = dot(pg[...], w_self[...], NT)
     esum[other_rows, :] = jnp.zeros((512, 256), F32)
-    c_edge = to_other(esum.at[other_rows, :], erecv, 9)
+    c_edge = to_other(esend, erecv, 9)
 
     def edge_block(t, carry):
         blk = block_of(t)
 
-        @pl.when(t == 0)
-        def _():
-            reduce_line()
-
-        @pl.when(t == 1)
-        def _():
-            gather_plane()
-
-        @pl.when(t == 3)
-        def _():
-            gather_cores()
-
+        stages_at(t, 4)
         wait_block(t, recv_b, br_sem)
         part = recv_b[rows_at(blk * BLOCK, BLOCK, BLOCK), :]
         esum[other_rows, :] += dot(at[blk, other_rows, :], part)
 
         @pl.when(t == 3)
         def _():
+            esend[...] = esum[other_rows, :].astype(CT)
             c_edge.start()
 
         esum[own_rows, :] += dot(at[blk, own_rows, :], part)
@@ -361,13 +378,24 @@
 
     lax.fori_loop(0, 4, edge_block, 0)
 
-    c_bias.wait_recv()
-    c_ag.wait_recv()
-    gself[...] = ag[0].reshape(256, 256)
-    gneigh[...] = ag[1].reshape(256, 256)
-    gbias[...] = (b2[0] + b2[1]) * scale
-    c_edge.wait_recv()
-    igrad[...] = (esum[own_rows, :] + erecv[...]).astype(BF)
+    def write_grads():
+        c_bias.wait_recv()
+        c_ag.wait_recv()
+        gself[...] = ag[0].astype(F32).reshape(256, 256)
+        gneigh[...] = ag[1].astype(F32).reshape(256, 256)
+        gbias[...] = (b2[0] + b2[1]) * scale
+        for store in stores[2:]:
+            store.start()
+
+    def write_input_grad():
+        c_edge.wait_recv()
+        igrad[...] = (esum[own_rows, :] + erecv[...]).astype(BF)
+        stores[1].start()
+
+    write_grads()
+    write_input_grad()
+    for store in stores:
+        store.wait()
 
     for copy in (c_src, c_slot, c_feat, c_deg, c_sum, c_mg, c_term, c_bias, c_ag, c_edge):
         copy.wait_send()
@@ -392,7 +420,7 @@
     sent(bb, 15, ar_send.at[1])
     sent(zr, 7, ar_send.at[2])
     sent(bz, 7, ar_send.at[3])
-    sent(rs, 15, ar_send.at[4])
+    sent(ag.at[0], 15, ar_send.at[4])
 
 
 def write_out(*refs):
@@ -406,9 +434,13 @@
 
 
 def shards(features, w_self, w_neigh, bias_vector, upstream, sources, edge_slots, mirror_rows):
-    vmem = pl.BlockSpec(memory_space=pltpu.VMEM)
     hbm = pl.BlockSpec(memory_space=pltpu.HBM)
     scratch = [
+        pltpu.VMEM((512, 256), BF),
+        pltpu.VMEM((512, 256), BF),
+        pltpu.VMEM((256, 256), F32),
+        pltpu.VMEM((256, 256), F32),
+        pltpu.VMEM((1, 256), F32),
         pltpu.VMEM((256, 256), BF),
         pltpu.VMEM((256, 256), BF),
         pltpu.VMEM((1, 256), F32),
@@ -428,32 +460,37 @@
         pltpu.VMEM((4, BLOCK, 1024), BF),
         pltpu.VMEM((4, 1024, BLOCK), BF),
         pltpu.VMEM((1024, 256), F32),
-        pltpu.VMEM((512, 256), F32),
-        pltpu.VMEM((1024, 128), F32),
+        pltpu.VMEM((512, 256), CT),
+        pltpu.VMEM((512, 256), CT),
+        pltpu.VMEM((1024, 256), F32),
+        pltpu.VMEM((512, 128), F32),
         pltpu.VMEM((512, 128), F32),
         pltpu.VMEM((1024, 256), BF),
         pltpu.VMEM((1024, 256), BF),
         pltpu.VMEM((1024, 256), BF),
         pltpu.VMEM((1024, 256), F32),
-        pltpu.VMEM((512, 256), F32),
+        pltpu.VMEM((512, 256), CT),
+        pltpu.VMEM((512, 256), CT),
         pltpu.VMEM((512, 256), F32),
         pltpu.VMEM((512, 256), BF),
         pltpu.VMEM((512, 256), BF),
         pltpu.VMEM((2, 256, 256), F32),
         pltpu.VMEM((256, 256), F32),
-        pltpu.VMEM((16, 16, 256), F32),
-        pltpu.VMEM((8, 16, 256), F32),
-        pltpu.VMEM((2, 16, 16, 256), F32),
+        pltpu.VMEM((256, 256), RT),
+        pltpu.VMEM((16, 16, 256), RT),
+        pltpu.VMEM((8, 16, 256), RT),
+        pltpu.VMEM((2, 16, 16, 256), GT),
         pltpu.VMEM((16, 1, 256), F32),
         pltpu.VMEM((8, 1, 256), F32),
         pltpu.VMEM((2, 1, 256), F32),
         pltpu.SemaphoreType.DMA((8,)),
+        pltpu.SemaphoreType.DMA((5,)),
         pltpu.SemaphoreType.DMA((10,)),
         pltpu.SemaphoreType.DMA((10,)),
         pltpu.SemaphoreType.DMA,
         pltpu.SemaphoreType.DMA((4,)),
         pltpu.SemaphoreType.DMA,
-        pltpu.SemaphoreType.DMA,
+        pltpu.SemaphoreType.DMA((4,)),
         pltpu.SemaphoreType.DMA,
         pltpu.SemaphoreType.DMA((4,)),
         pltpu.SemaphoreType.DMA((5,)),
@@ -470,7 +507,7 @@
         kernel,
         out_shape=shapes,
         in_specs=[hbm] * 8,
-        out_specs=(vmem,) * 5,
+        out_specs=(hbm,) * 5,
         scratch_shapes=scratch,
         compiler_params=pltpu.CompilerParams(
             collective_id=0, has_side_effects=True, vmem_limit_bytes=63 * 2**20
@@ -483,7 +520,7 @@
     hidden, igrad, gself, gneigh, gbias = pl.pallas_call(
         write_out,
         out_shape=shapes,
-        in_specs=[vmem] * 5,
+        in_specs=[pl.BlockSpec(memory_space=pltpu.VMEM)] * 5,
         out_specs=(hbm,) * 5,
         scratch_shapes=[pltpu.SemaphoreType.DMA((5,))],
         name="write_out",

time: 72.4 us -> 65.9 us (0.910)
  Pallas kernels: 71.6 us -> 65.1 us
    pallas_call x2, Pallas kernels: 71.6 us -> 65.1 us  [the longest x1 62.9 us: shards(): pl.pallas_call(kernel, out_shape=shapes, in_specs=[hbm] * 8, out_specs=(h...]
where the time goes in v3:
time: 65.9 us; the launch traced here: 65.8 us
  Pallas kernels  65.1 us (99%)
    pallas_call x1, Pallas kernels, shards(): pl.pallas_call(kernel, out_shape=shapes, in_specs=[hbm] * 8, out_specs=(h...  62.9 us
    pallas_call x1, Pallas kernels, shards(): pl.pallas_call(write_out, out_shape=shapes, in_specs=[pl.BlockSpec(memory...  2.2 us

profile of v3, /device:TPU:1, one launch (start us, length us, event | category | flops | bytes accessed | tf_op | source)
XLA Modules:
  0.0 65.8 jit_solution(15035410555746664921)
XLA Ops:
  0.6 62.9 %sage_layer.1 = (bf16[512,256]{1,0:T(8,128)(2,1)}, bf16[512,256]{1,0:T(8,128)(2,1)}, f32[256,256]{1,0:T(8,128)}, f32[256,256]{1,0:T(8,128)}, f32[1,256]{1,0:T(1,128)}) custom-call(bf16[512,256]{1,0:T(8,128)(2,1)} %feat_h.1, bf16[256,256]{1,0:T(8,128)(2,1)} %w_self_h.1, bf16[256,256]{1,0:T(8,128)(2,1)} %w_neigh_h.1, f32[1,256]{1,0:T(1,128)} %bitcast.10, ...), custom_call_target="tpu_custom_call" | custom-call | tf_op jit(solution)/shard_map/sage_layer/pallas_call | solution.py:506
  63.6 2.2 %write_out.1 = (bf16[512,256]{1,0:T(8,128)(2,1)}, bf16[512,256]{1,0:T(8,128)(2,1)}, f32[256,256]{1,0:T(8,128)}, f32[256,256]{1,0:T(8,128)}, f32[1,256]{1,0:T(1,128)}) custom-call(bf16[512,256]{1,0:T(8,128)(2,1)} %get-tuple-element.15.refs_0_, bf16[512,256]{1,0:T(8,128)(2,1)} %get-tuple-element.16.refs_1_, f32[256,256]{1,0:T(8,128)} %get-tuple-element.17.refs_2_, ...), custom_call_target="tpu_custom_call" | custom-call | tf_op jit(solution)/shard_map/write_out/pallas_call | solution.py:520

commit v4 on v3

--- a/solution.py
+++ b/solution.py
@@ -23,7 +23,7 @@
 RT = BF
 GT = BF
 CT = BF
-AT = (0, 1, 2, 6)
+AT = (0, 1, 3, 6)
 
 
 def dot(a, b, dims=NN):
@@ -266,6 +266,7 @@
         pre_grad = up[rows, :].astype(F32) * (gate + pre * gate * (1.0 - gate))
         pre_grad = pre_grad.astype(BF)
         mg[mine, :] = (dot(pre_grad, w_neigh[...], NT) / divisor).astype(BF)
+        to_other(mg.at[mine, :], mg.at[mine, :], 5).start()
         hidden[rows, :] = (pre * gate).astype(BF)
         mn[rows, :] = mean
         pg[rows, :] = pre_grad
@@ -274,7 +275,6 @@
     lax.fori_loop(0, 4, dense_block, 0)
     stores[0].start()
     c_mg = to_other(mg.at[own_rows, :], mg.at[own_rows, :], 5)
-    c_mg.start()
     term[0] = dot(fall[own_rows, :], pg[...], TN)
     term[1] = dot(mn[...], pg[...], TN)
     c_term = to_other(term.at[o], trecv, 6)

time: 65.9 us -> 65.5 us (level)
  no operation moved by 1% of the time
where the time goes in v4:
time: 65.5 us; the launch traced here: 65.4 us
  Pallas kernels  64.7 us (99%)
    pallas_call x1, Pallas kernels, shards(): pl.pallas_call(kernel, out_shape=shapes, in_specs=[hbm] * 8, out_specs=(h...  62.5 us
    pallas_call x1, Pallas kernels, shards(): pl.pallas_call(write_out, out_shape=shapes, in_specs=[pl.BlockSpec(memory...  2.2 us

profile of v4, /device:TPU:1, one launch (start us, length us, event | category | flops | bytes accessed | tf_op | source)
XLA Modules:
  0.0 65.4 jit_solution(2542051658194640065)
XLA Ops:
  0.6 62.5 %sage_layer.1 = (bf16[512,256]{1,0:T(8,128)(2,1)}, bf16[512,256]{1,0:T(8,128)(2,1)}, f32[256,256]{1,0:T(8,128)}, f32[256,256]{1,0:T(8,128)}, f32[1,256]{1,0:T(1,128)}) custom-call(bf16[512,256]{1,0:T(8,128)(2,1)} %feat_h.1, bf16[256,256]{1,0:T(8,128)(2,1)} %w_self_h.1, bf16[256,256]{1,0:T(8,128)(2,1)} %w_neigh_h.1, f32[1,256]{1,0:T(1,128)} %bitcast.10, ...), custom_call_target="tpu_custom_call" | custom-call | tf_op jit(solution)/shard_map/sage_layer/pallas_call | solution.py:506
  63.2 2.2 %write_out.1 = (bf16[512,256]{1,0:T(8,128)(2,1)}, bf16[512,256]{1,0:T(8,128)(2,1)}, f32[256,256]{1,0:T(8,128)}, f32[256,256]{1,0:T(8,128)}, f32[1,256]{1,0:T(1,128)}) custom-call(bf16[512,256]{1,0:T(8,128)(2,1)} %get-tuple-element.15.refs_0_, bf16[512,256]{1,0:T(8,128)(2,1)} %get-tuple-element.16.refs_1_, f32[256,256]{1,0:T(8,128)} %get-tuple-element.17.refs_2_, ...), custom_call_target="tpu_custom_call" | custom-call | tf_op jit(solution)/shard_map/write_out/pallas_call | solution.py:520
